TPU v7x, 256 devices: a whole 4x4x8 slice. The times are simulated.
256 devices in a mesh: base: 32 (over x, y, core), band: 8 (over z).
Axes of the slice: x: 4, y: 4, z: 8, core: 2. Of those that a mesh axis runs over, the one named last changes fastest.
Arguments:
- visibilities: float32 [65536, 2, 128], P(('base', 'band')), may hold values from -6 to 6
- coords: float32 [65536, 2, 8], P(('base', 'band')), may hold values from -11.2 to 11.2
- chan_scale: float32 [16], replicated, may hold values from 0.9 to 1.1
- taper_gain: float32 [32, 32], replicated, may hold values from 0.25 to 1
- owner_base: int32 [65536, 1], P(('base', 'band')), may hold values from 0 to 31; in each aligned block of 256 rows (0 to 255, 256 to 511, ...) at most 16 rows name the same one
- tile_cell: int32 [65536], P(('base', 'band')), may hold values from 0 to 255
Outputs:
- image: float32 [2, 8192, 8192], P(None, ('base', 'band'))
Inputs may be any that keep to these rules, and one draw needn't show every extreme that they name: `owner_base`: among the 256 baselines of one device no value occurs more than 16 times, and in every draw some device has a value exactly 16 times.
All inputs are finite; a program needn't handle non-finite values.
Results may differ from a plain program's by a relative error of at most 0.0003.
Values sent between devices are 32-bit elements; how exact they have to be, the bound alone decides.
A program may use at most 128 MiB of HBM per device.

v0:
```python
import math
import jax
import jax.numpy as jnp
from jax import lax
from jax.sharding import PartitionSpec as P

G = 8192
two_pi = 2.0 * math.pi
exact = lax.Precision.HIGHEST


def phase_table(length, direction):
    indices = jnp.arange(length, dtype=jnp.int32)
    product = indices[:, None] * indices[None, :] % length
    angle = direction * two_pi / length * product.astype(jnp.float32)
    return (jnp.cos(angle), jnp.sin(angle))


def grid_block(samples, places, chan_scale, taper_gain):
    number = samples.shape[0]
    extent = taper_gain.shape[0]
    time_count = places.shape[2]
    sample_count = time_count * chan_scale.shape[0]
    offsets = (jnp.arange(extent, dtype=jnp.float32) - extent // 2) / extent
    u_pos = (places[:, 0, :, None] * chan_scale[None, None, :]).reshape(number, sample_count)
    v_pos = (places[:, 1, :, None] * chan_scale[None, None, :]).reshape(number, sample_count)
    angle_y = two_pi * offsets[None, :, None] * v_pos[:, None, :]
    angle_x = two_pi * offsets[None, :, None] * u_pos[:, None, :]
    cos_y = jnp.cos(angle_y)
    sin_y = jnp.sin(angle_y)
    cos_x = jnp.cos(angle_x)
    sin_x = jnp.sin(angle_x)
    real_in = samples[:, 0:1, :]
    imag_in = samples[:, 1:2, :]
    left_re = real_in * cos_y - imag_in * sin_y
    left_im = real_in * sin_y + imag_in * cos_y

    def pairwise(first_arr, second_arr):
        return jnp.einsum("nyv,nxv->nyx", first_arr, second_arr, precision=exact)

    pix_re = (pairwise(left_re, cos_x) - pairwise(left_im, sin_x)) * taper_gain
    pix_im = (pairwise(left_re, sin_x) + pairwise(left_im, cos_x)) * taper_gain
    f_cos, f_sin = phase_table(extent, 1.0)

    def along_x(values, table):
        return jnp.einsum("nyx,xk->nyk", values, table, precision=exact)

    def along_y(values, table):
        return jnp.einsum("yk,nyx->nkx", table, values, precision=exact)

    q_re = along_x(pix_re, f_cos) + along_x(pix_im, f_sin)
    q_im = along_x(pix_im, f_cos) - along_x(pix_re, f_sin)
    t_re = along_y(q_re, f_cos) + along_y(q_im, f_sin)
    t_im = along_y(q_im, f_cos) - along_y(q_re, f_sin)
    factor = 1.0 / (extent * math.sqrt(sample_count))
    return jnp.stack([t_re, t_im], axis=1).reshape(number, 2, extent * extent) * factor


def make_tiles(samples, places, chan_scale, taper_gain):
    number = samples.shape[0]
    block_size = math.gcd(number, 64)
    blocks = number // block_size

    def one_block(pieces):
        return grid_block(pieces[0], pieces[1], chan_scale, taper_gain)

    result = lax.map(
        one_block,
        (
            samples.reshape(blocks, block_size, 2, samples.shape[2]),
            places.reshape(blocks, block_size, 2, places.shape[2]),
        ),
    )
    return result.reshape(number, 2, result.shape[3])


def dft_last(real_part, imag_part):
    row_count = real_part.shape[0]
    length = real_part.shape[1]
    first_len = 2 ** ((length.bit_length() - 1) // 2)
    second_len = length // first_len
    cos_one, sin_one = phase_table(first_len, 1.0)
    cos_two, sin_two = phase_table(second_len, 1.0)
    real_in = real_part.reshape(row_count, first_len, second_len)
    imag_in = imag_part.reshape(row_count, first_len, second_len)

    def mix_first(values, table):
        return jnp.einsum("pab,ak->pkb", values, table, precision=exact)

    y_re = mix_first(real_in, cos_one) - mix_first(imag_in, sin_one)
    y_im = mix_first(real_in, sin_one) + mix_first(imag_in, cos_one)
    first_ids = jnp.arange(first_len, dtype=jnp.int32)
    second_ids = jnp.arange(second_len, dtype=jnp.int32)
    turns = first_ids[:, None] * second_ids[None, :] % length
    twist = two_pi / length * turns.astype(jnp.float32)
    twist_cos = jnp.cos(twist)
    twist_sin = jnp.sin(twist)
    z_re = y_re * twist_cos - y_im * twist_sin
    z_im = y_re * twist_sin + y_im * twist_cos

    def mix_second(values, table):
        return jnp.einsum("pkb,bm->pmk", values, table, precision=exact)

    out_re = mix_second(z_re, cos_two) - mix_second(z_im, sin_two)
    out_im = mix_second(z_re, sin_two) + mix_second(z_im, cos_two)
    return (out_re.reshape(row_count, length), out_im.reshape(row_count, length))


def shards(visibilities, coords, chan_scale, taper_gain, owner_base, tile_cell):
    n_base = lax.axis_size("base")
    n_band = lax.axis_size("band")
    slot_count = visibilities.shape[0]
    extent = taper_gain.shape[0]
    area = extent * extent
    capacity = 2 * slot_count // n_base
    buffer_len = capacity * n_base
    owners = owner_base[:, 0]
    onehot = (owners[:, None] == jnp.arange(n_base, dtype=jnp.int32)[None, :]).astype(jnp.int32)
    before = jnp.cumsum(onehot, axis=0) - onehot
    rank_in = jnp.sum(before * onehot, axis=1)
    target = rank_in * n_base + owners
    cell_slots = jnp.zeros((buffer_len,), jnp.float32).at[target].set(tile_cell.astype(jnp.float32))
    cell_slots = cell_slots.reshape(capacity, n_base)
    tiles = make_tiles(visibilities, coords, chan_scale, taper_gain)
    packed = jnp.zeros((buffer_len, 2, area), jnp.float32).at[target].set(tiles)
    packed = packed.reshape(capacity, n_base, 2, area)
    arrived, arrived_cells = (
        lax.all_to_all(packed, "base", split_axis=1, concat_axis=1, tiled=True),
        lax.all_to_all(cell_slots, "base", split_axis=1, concat_axis=1, tiled=True),
    )
    row_tiles = G // (extent * n_band)
    col_tiles = G // (extent * n_base)
    segment_ids = arrived_cells.reshape(buffer_len).astype(jnp.int32)
    summed = jax.ops.segment_sum(
        arrived.reshape(buffer_len, 2 * area), segment_ids, num_segments=row_tiles * col_tiles
    )
    uv_grid = summed.reshape(row_tiles, col_tiles, 2, extent, extent).transpose(2, 0, 3, 1, 4)
    uv_grid = uv_grid.reshape(2, row_tiles * extent, col_tiles * extent)
    row_major = lax.all_to_all(uv_grid, "base", split_axis=1, concat_axis=2, tiled=True)
    row_re, row_im = dft_last(row_major[0], row_major[1])
    returned = lax.all_to_all(
        jnp.stack([row_re, row_im]), "base", split_axis=2, concat_axis=1, tiled=True
    )
    flipped = jnp.transpose(returned, (0, 2, 1))
    col_major = lax.all_to_all(flipped, "band", split_axis=1, concat_axis=2, tiled=True)
    col_re, col_im = dft_last(col_major[0], col_major[1])
    return jnp.stack([col_re, col_im]) * (1.0 / G)


def solution(mesh):
    placed = (
        P(("base", "band"), None, None),
        P(("base", "band"), None, None),
        P(),
        P(),
        P(("base", "band"), None),
        P(("base", "band")),
    )
    return jax.shard_map(
        shards,
        mesh=mesh,
        in_specs=placed,
        out_specs=P(None, ("base", "band"), None),
        check_vma=False,
    )
```

profile of v0, /device:TPU:1, one launch (start us, length us, event | category | flops | bytes accessed | tf_op | source)
XLA Modules:
  0.0 582.1 jit_solution(8600578806524166067)
XLA Ops:
  3.6 1.4 scatter_custom_fusion
  5.8 8.6 %all-to-all-start = ((f32[16,32,1]{0,2,1:T(1,128)}), f32[16,32,1]{0,2,1:T(1,128)S(1)}, u32[]{:S(2)}, u32[]{:S(2)}) async-start(f32[16,32,1]{0,2,1:T(1,128)} %copy.184), calls=%async_computation | async-start | bytes 32768 | tf_op jit(solution)/shard_map/all_to_all | solution.py:129
  15.2 196.9 %while.12 = (s32[]{:T(128)}, f32[4,64,2,1024]{3,1,0,2:T(8,128)}, f32[4,64,2,128]{3,2,1,0:T(2,128)}, f32[4,64,2,8]{1,0,3,2:T(4,128)S(1)}, f32[16]{0:T(128)}, /*index=5*/f32[32,32]{1,0:T(8,128)}, s32[]{:T(128)}) while((s32[]{:T(128)}, f32[4,64,2,1024]{3,1,0,2:T(8,128)}, f32[4,64,2,128]{3,2,1,0:T(2,128)}, f32[4,64,2,8]{1,0,3,2:T(4,128)S(1)}, ...), condition=%wide.region_5.6_spmd, body=%wide.region_4.5_spmd.sunk | while | flops 610140224 | bytes 13221169 | solution.py:67
  17.4 8.9 %fusion.319 = f32[64,32,32]{2,1,0:T(8,128)S(1)} fusion(f32[64,128]{1,0:T(8,128)S(1)} %copy.248, f32[64,128]{1,0:T(8,128)S(1)} %get-tuple-element.192, f32[64,128]{1,0:T(8,128)S(1)} %copy.250, f32[32]{0:T(128)S(1)} %add_multiply_fusion.2, f32[64,128]{1,0:T(8,128)S(1)} %get-tuple-element.194), kind=kOutput, calls=%fused_computation.12.clone.1 | convolution fusion | flops 101974016 | bytes 393344 | tf_op jit(solution)/shard_map/while/body/eval_jaxpr/nyv,nxv->nyx/dot_general | solution.py:39
  26.3 9.4 %fusion.320 = f32[64,32,32]{2,1,0:T(8,128)S(1)} fusion(f32[64,32,32]{2,1,0:T(8,128)S(1)} %fusion.319, f32[32,32]{1,0:T(8,128)S(1)} %copy-done.2, f32[64,128]{1,0:T(8,128)S(1)} %copy.248, f32[64,128]{1,0:T(8,128)S(1)} %get-tuple-element.192, f32[64,128]{1,0:T(8,128)S(1)} %copy.250, f32[32]{0:T(128)S(1)} %add_multiply_fusion.2, ...), kind=kOutput, calls=%fused_computation.18.clone.1 | convolution fusion | flops 102105088 | bytes 659584 | tf_op jit(solution)/shard_map/while/body/eval_jaxpr/nyv,nxv->nyx/dot_general | solution.py:39
  37.0 9.0 %fusion.316 = f32[64,32,32]{2,1,0:T(8,128)S(1)} fusion(f32[64,128]{1,0:T(8,128)S(1)} %copy.248, f32[64,128]{1,0:T(8,128)S(1)} %get-tuple-element.192, f32[64,128]{1,0:T(8,128)S(1)} %copy.250, f32[32]{0:T(128)S(1)} %add_multiply_fusion.2, f32[64,128]{1,0:T(8,128)S(1)} %get-tuple-element.194), kind=kOutput, calls=%fused_computation.11.clone.1 | convolution fusion | flops 101974016 | bytes 393344 | tf_op jit(solution)/shard_map/while/body/eval_jaxpr/nyv,nxv->nyx/dot_general | solution.py:39
  46.0 9.1 %fusion.317 = f32[64,32,32]{2,1,0:T(8,128)S(1)} fusion(f32[64,32,32]{2,1,0:T(8,128)S(1)} %fusion.316, f32[32,32]{1,0:T(8,128)S(1)} %copy-done.2, f32[64,128]{1,0:T(8,128)S(1)} %copy.248, f32[64,128]{1,0:T(8,128)S(1)} %get-tuple-element.192, f32[64,128]{1,0:T(8,128)S(1)} %copy.250, f32[32]{0:T(128)S(1)} %add_multiply_fusion.2, ...), kind=kOutput, calls=%fused_computation.17.clone.1 | convolution fusion | flops 102105088 | bytes 659584 | tf_op jit(solution)/shard_map/while/body/eval_jaxpr/nyv,nxv->nyx/dot_general | solution.py:39
  65.8 8.9 %fusion.319 = f32[64,32,32]{2,1,0:T(8,128)S(1)} fusion(f32[64,128]{1,0:T(8,128)S(1)} %copy.248, f32[64,128]{1,0:T(8,128)S(1)} %get-tuple-element.192, f32[64,128]{1,0:T(8,128)S(1)} %copy.250, f32[32]{0:T(128)S(1)} %add_multiply_fusion.2, f32[64,128]{1,0:T(8,128)S(1)} %get-tuple-element.194), kind=kOutput, calls=%fused_computation.12.clone.1 | convolution fusion | flops 101974016 | bytes 393344 | tf_op jit(solution)/shard_map/while/body/eval_jaxpr/nyv,nxv->nyx/dot_general | solution.py:39
  74.6 9.1 %fusion.320 = f32[64,32,32]{2,1,0:T(8,128)S(1)} fusion(f32[64,32,32]{2,1,0:T(8,128)S(1)} %fusion.319, f32[32,32]{1,0:T(8,128)S(1)} %copy-done.2, f32[64,128]{1,0:T(8,128)S(1)} %copy.248, f32[64,128]{1,0:T(8,128)S(1)} %get-tuple-element.192, f32[64,128]{1,0:T(8,128)S(1)} %copy.250, f32[32]{0:T(128)S(1)} %add_multiply_fusion.2, ...), kind=kOutput, calls=%fused_computation.18.clone.1 | convolution fusion | flops 102105088 | bytes 659584 | tf_op jit(solution)/shard_map/while/body/eval_jaxpr/nyv,nxv->nyx/dot_general | solution.py:39
  84.9 9.1 %fusion.316 = f32[64,32,32]{2,1,0:T(8,128)S(1)} fusion(f32[64,128]{1,0:T(8,128)S(1)} %copy.248, f32[64,128]{1,0:T(8,128)S(1)} %get-tuple-element.192, f32[64,128]{1,0:T(8,128)S(1)} %copy.250, f32[32]{0:T(128)S(1)} %add_multiply_fusion.2, f32[64,128]{1,0:T(8,128)S(1)} %get-tuple-element.194), kind=kOutput, calls=%fused_computation.11.clone.1 | convolution fusion | flops 101974016 | bytes 393344 | tf_op jit(solution)/shard_map/while/body/eval_jaxpr/nyv,nxv->nyx/dot_general | solution.py:39
  94.0 9.3 %fusion.317 = f32[64,32,32]{2,1,0:T(8,128)S(1)} fusion(f32[64,32,32]{2,1,0:T(8,128)S(1)} %fusion.316, f32[32,32]{1,0:T(8,128)S(1)} %copy-done.2, f32[64,128]{1,0:T(8,128)S(1)} %copy.248, f32[64,128]{1,0:T(8,128)S(1)} %get-tuple-element.192, f32[64,128]{1,0:T(8,128)S(1)} %copy.250, f32[32]{0:T(128)S(1)} %add_multiply_fusion.2, ...), kind=kOutput, calls=%fused_computation.17.clone.1 | convolution fusion | flops 102105088 | bytes 659584 | tf_op jit(solution)/shard_map/while/body/eval_jaxpr/nyv,nxv->nyx/dot_general | solution.py:39
  113.7 8.9 %fusion.319 = f32[64,32,32]{2,1,0:T(8,128)S(1)} fusion(f32[64,128]{1,0:T(8,128)S(1)} %copy.248, f32[64,128]{1,0:T(8,128)S(1)} %get-tuple-element.192, f32[64,128]{1,0:T(8,128)S(1)} %copy.250, f32[32]{0:T(128)S(1)} %add_multiply_fusion.2, f32[64,128]{1,0:T(8,128)S(1)} %get-tuple-element.194), kind=kOutput, calls=%fused_computation.12.clone.1 | convolution fusion | flops 101974016 | bytes 393344 | tf_op jit(solution)/shard_map/while/body/eval_jaxpr/nyv,nxv->nyx/dot_general | solution.py:39
  122.6 9.1 %fusion.320 = f32[64,32,32]{2,1,0:T(8,128)S(1)} fusion(f32[64,32,32]{2,1,0:T(8,128)S(1)} %fusion.319, f32[32,32]{1,0:T(8,128)S(1)} %copy-done.2, f32[64,128]{1,0:T(8,128)S(1)} %copy.248, f32[64,128]{1,0:T(8,128)S(1)} %get-tuple-element.192, f32[64,128]{1,0:T(8,128)S(1)} %copy.250, f32[32]{0:T(128)S(1)} %add_multiply_fusion.2, ...), kind=kOutput, calls=%fused_computation.18.clone.1 | convolution fusion | flops 102105088 | bytes 659584 | tf_op jit(solution)/shard_map/while/body/eval_jaxpr/nyv,nxv->nyx/dot_general | solution.py:39
  133.0 9.3 %fusion.316 = f32[64,32,32]{2,1,0:T(8,128)S(1)} fusion(f32[64,128]{1,0:T(8,128)S(1)} %copy.248, f32[64,128]{1,0:T(8,128)S(1)} %get-tuple-element.192, f32[64,128]{1,0:T(8,128)S(1)} %copy.250, f32[32]{0:T(128)S(1)} %add_multiply_fusion.2, f32[64,128]{1,0:T(8,128)S(1)} %get-tuple-element.194), kind=kOutput, calls=%fused_computation.11.clone.1 | convolution fusion | flops 101974016 | bytes 393344 | tf_op jit(solution)/shard_map/while/body/eval_jaxpr/nyv,nxv->nyx/dot_general | solution.py:39
  142.2 9.1 %fusion.317 = f32[64,32,32]{2,1,0:T(8,128)S(1)} fusion(f32[64,32,32]{2,1,0:T(8,128)S(1)} %fusion.316, f32[32,32]{1,0:T(8,128)S(1)} %copy-done.2, f32[64,128]{1,0:T(8,128)S(1)} %copy.248, f32[64,128]{1,0:T(8,128)S(1)} %get-tuple-element.192, f32[64,128]{1,0:T(8,128)S(1)} %copy.250, f32[32]{0:T(128)S(1)} %add_multiply_fusion.2, ...), kind=kOutput, calls=%fused_computation.17.clone.1 | convolution fusion | flops 102105088 | bytes 659584 | tf_op jit(solution)/shard_map/while/body/eval_jaxpr/nyv,nxv->nyx/dot_general | solution.py:39
  161.8 8.9 %fusion.319 = f32[64,32,32]{2,1,0:T(8,128)S(1)} fusion(f32[64,128]{1,0:T(8,128)S(1)} %copy.248, f32[64,128]{1,0:T(8,128)S(1)} %get-tuple-element.192, f32[64,128]{1,0:T(8,128)S(1)} %copy.250, f32[32]{0:T(128)S(1)} %add_multiply_fusion.2, f32[64,128]{1,0:T(8,128)S(1)} %get-tuple-element.194), kind=kOutput, calls=%fused_computation.12.clone.1 | convolution fusion | flops 101974016 | bytes 393344 | tf_op jit(solution)/shard_map/while/body/eval_jaxpr/nyv,nxv->nyx/dot_general | solution.py:39
  170.6 9.3 %fusion.320 = f32[64,32,32]{2,1,0:T(8,128)S(1)} fusion(f32[64,32,32]{2,1,0:T(8,128)S(1)} %fusion.319, f32[32,32]{1,0:T(8,128)S(1)} %copy-done.2, f32[64,128]{1,0:T(8,128)S(1)} %copy.248, f32[64,128]{1,0:T(8,128)S(1)} %get-tuple-element.192, f32[64,128]{1,0:T(8,128)S(1)} %copy.250, f32[32]{0:T(128)S(1)} %add_multiply_fusion.2, ...), kind=kOutput, calls=%fused_computation.18.clone.1 | convolution fusion | flops 102105088 | bytes 659584 | tf_op jit(solution)/shard_map/while/body/eval_jaxpr/nyv,nxv->nyx/dot_general | solution.py:39
  181.2 9.0 %fusion.316 = f32[64,32,32]{2,1,0:T(8,128)S(1)} fusion(f32[64,128]{1,0:T(8,128)S(1)} %copy.248, f32[64,128]{1,0:T(8,128)S(1)} %get-tuple-element.192, f32[64,128]{1,0:T(8,128)S(1)} %copy.250, f32[32]{0:T(128)S(1)} %add_multiply_fusion.2, f32[64,128]{1,0:T(8,128)S(1)} %get-tuple-element.194), kind=kOutput, calls=%fused_computation.11.clone.1 | convolution fusion | flops 101974016 | bytes 393344 | tf_op jit(solution)/shard_map/while/body/eval_jaxpr/nyv,nxv->nyx/dot_general | solution.py:39
  190.2 9.1 %fusion.317 = f32[64,32,32]{2,1,0:T(8,128)S(1)} fusion(f32[64,32,32]{2,1,0:T(8,128)S(1)} %fusion.316, f32[32,32]{1,0:T(8,128)S(1)} %copy-done.2, f32[64,128]{1,0:T(8,128)S(1)} %copy.248, f32[64,128]{1,0:T(8,128)S(1)} %get-tuple-element.192, f32[64,128]{1,0:T(8,128)S(1)} %copy.250, f32[32]{0:T(128)S(1)} %add_multiply_fusion.2, ...), kind=kOutput, calls=%fused_computation.17.clone.1 | convolution fusion | flops 102105088 | bytes 659584 | tf_op jit(solution)/shard_map/while/body/eval_jaxpr/nyv,nxv->nyx/dot_general | solution.py:39
  212.1 3.2 copy.190
  215.4 3.0 broadcast_in_dim.11
  218.4 26.5 %scatter_fusion = f32[512,2,1024]{2,1,0:T(2,128)} fusion(f32[512,2,1024]{2,1,0:T(2,128)} %broadcast_in_dim.11, s32[256]{0:T(256)S(1)} %bitcast.240, f32[256,2,1024]{2,1,0:T(2,128)S(1)} %copy.190), kind=kCustom, calls=%fused_computation.1 | custom fusion | bytes 6292480 | tf_op jit(solution)/shard_map/scatter | solution.py:125
  244.9 6.6 %copy.191 = f32[16,32,2,1024]{3,2,0,1:T(2,128)} copy(f32[16,32,2,1024]{3,2,1,0:T(2,128)} %bitcast.226) | data formatting | bytes 8388608 | tf_op jit(solution)/shard_map/reshape | solution.py:126
  251.6 7.8 %all-to-all-start.1 = ((f32[16,32,2,1024]{3,2,0,1:T(2,128)}), f32[16,32,2,1024]{3,2,0,1:T(2,128)}, u32[]{:S(2)}, u32[]{:S(2)}) async-start(f32[16,32,2,1024]{3,2,0,1:T(2,128)} %copy.191), calls=%async_computation.1 | async-start | bytes 8388608 | tf_op jit(solution)/shard_map/all_to_all | solution.py:128
  259.6 51.9 %all-to-all-done.1 = f32[16,32,2,1024]{3,2,0,1:T(2,128)} async-done(((f32[16,32,2,1024]{3,2,0,1:T(2,128)}), f32[16,32,2,1024]{3,2,0,1:T(2,128)}, u32[]{:S(2)}, u32[]{:S(2)}) %all-to-all-start.1) | async-done | bytes 4194336 | tf_op jit(solution)/shard_map/all_to_all | solution.py:128
  311.4 4.3 copy.192
  315.8 3.9 copy.220
  319.7 8.9 %scatter_custom_fusion.2 = f32[256,2048]{1,0:T(8,128)S(1)} fusion(s32[512]{0:T(512)S(1)} %reshape.227, f32[512,2048]{1,0:T(8,128)} %bitcast.232, f32[]{:T(128)} %constant.129.clone.1), kind=kCustom, calls=%fused_computation.148 | custom fusion | flops 1048576 | bytes 2097664 | tf_op jit(solution)/shard_map/scatter-add | solution.py:134
  328.6 5.2 reshape.207
  333.8 14.3 %copy.211 = f32[2,32,32,8,32]{4,3,0,2,1:T(8,128)} copy(f32[2,32,32,8,32]{4,2,0,3,1:T(8,128)} %bitcast.225) | data formatting | bytes 4194304 | tf_op jit(solution)/shard_map/reshape | solution.py:138
  348.1 7.7 %reshape.240 = f32[2,1024,256]{2,0,1:T(2,128)} reshape(f32[2,32,32,8,32]{4,3,0,2,1:T(8,128)} %copy.211) | data formatting | bytes 4194304 | tf_op jit(solution)/shard_map/reshape | solution.py:138
  355.8 7.4 %all-to-all-start.2 = ((f32[2,1024,256]{2,0,1:T(2,128)}), f32[2,1024,256]{2,0,1:T(2,128)S(1)}, u32[]{:S(2)}, u32[]{:S(2)}) async-start(f32[2,1024,256]{2,0,1:T(2,128)} %reshape.240), calls=%async_computation.2 | async-start | bytes 4194304 | tf_op jit(solution)/shard_map/all_to_all | solution.py:139
  363.4 28.0 %all-to-all-done.2 = f32[2,1024,256]{2,0,1:T(2,128)S(1)} async-done(((f32[2,1024,256]{2,0,1:T(2,128)}), f32[2,1024,256]{2,0,1:T(2,128)S(1)}, u32[]{:S(2)}, u32[]{:S(2)}) %all-to-all-start.2) | async-done | bytes 2097184 | tf_op jit(solution)/shard_map/all_to_all | solution.py:139
  392.4 1.2 fusion.155
  393.6 2.1 fusion.148
  397.6 1.2 convolution_add_fusion.5
  398.8 1.2 fusion.118
  400.1 2.2 fusion.116
  402.3 1.2 fusion.107
  403.5 1.9 copy.198
  405.5 2.3 stack_reshape.12
  407.8 3.4 fusion.106
  411.2 1.8 copy.199
  413.1 1.6 stack_reshape.13
  414.7 1.4 pad_maximum_fusion
  416.1 7.9 %copy.200 = f32[2,32,8192]{1,0,2:T(2,128)} copy(f32[2,32,8192]{2,1,0:T(8,128)S(1)} %pad_maximum_fusion) | data formatting | bytes 4194304 | tf_op jit(solution)/shard_map/stack | solution.py:142
  423.9 10.2 %reshape.246 = f32[32,1,16384]{2,1,0:T(1,128)S(1)} reshape(f32[8192,2,32]{2,1,0:T(2,128)} %bitcast.223) | data formatting | bytes 4194304
  434.1 32.4 %all_to_all.62 = f32[32,1,16384]{2,1,0:T(1,128)} all-to-all(f32[32,1,16384]{2,1,0:T(1,128)S(1)} %reshape.246), channel_id=1, replica_groups=mesh['base'=32,'band'=8] {'base'}, dimensions={0} | all-to-all | bytes 4194304 | tf_op jit(solution)/shard_map/all_to_all | solution.py:141
  467.0 7.4 %reduce.2 = f32[32,16384]{1,0:T(8,128)S(1)} reduce(f32[32,1,16384]{2,1,0:T(1,128)} %all_to_all.62, f32[]{:T(128)} %broadcast.405), dimensions={1}, to_apply=%all_to_all.50.reduce_sub_computation | reduce | bytes 4194308 | tf_op jit(solution)/shard_map/all_to_all | solution.py:141
  474.4 8.4 %reshape.247 = f32[8192,2,32]{2,1,0:T(2,128)} reshape(f32[32,16384]{1,0:T(8,128)S(1)} %reduce.2) | data formatting | bytes 4194304
  482.9 9.7 %copy.213 = f32[2,32,32,256]{3,1,2,0:T(8,128)S(1)} copy(f32[2,32,32,256]{1,0,3,2:T(2,128)} %bitcast.224) | data formatting | bytes 4194304 | tf_op jit(solution)/shard_map/all_to_all | solution.py:141
  492.6 2.3 copy.203
  495.0 60.2 %all_to_all.63 = f32[2,256,1024]{2,0,1:T(2,128)S(1)} all-to-all(f32[2,256,1024]{2,0,1:T(2,128)} %copy.203), channel_id=1, replica_groups=mesh['base'=32,'band'=8] {'band'}, dimensions={1} | all-to-all | bytes 4194304 | tf_op jit(solution)/shard_map/all_to_all | solution.py:145
  558.1 2.1 fusion.145
  562.2 1.2 convolution_add_fusion.3
  563.4 1.2 fusion.112
  564.6 2.2 fusion.110
  566.9 1.2 fusion.105
  568.1 1.9 copy.207
  570.0 2.3 stack_reshape.14
  572.3 3.4 fusion.104
  575.7 1.8 copy.208
  577.6 1.6 stack_reshape.15
  579.2 2.7 maximum_multiply_fusion.1
  (150 shorter events, 59.1 us)
Async XLA Ops:
  5.8 245.8 %all-to-all-start = ((f32[16,32,1]{0,2,1:T(1,128)}), f32[16,32,1]{0,2,1:T(1,128)S(1)}, u32[]{:S(2)}, u32[]{:S(2)}) async-start(f32[16,32,1]{0,2,1:T(1,128)} %copy.184), calls=%async_computation | async-start | bytes 32768 | tf_op jit(solution)/shard_map/all_to_all | solution.py:129
  15.5 10.8 %copy-start.2 = (f32[32,32]{1,0:T(8,128)S(1)}, f32[32,32]{1,0:T(8,128)}, u32[]{:S(2)}) copy-start(f32[32,32]{1,0:T(8,128)} %get-tuple-element.214) | copy-start | bytes 12292 | tf_op jit(solution)/shard_map/while
  63.8 10.8 %copy-start.2 = (f32[32,32]{1,0:T(8,128)S(1)}, f32[32,32]{1,0:T(8,128)}, u32[]{:S(2)}) copy-start(f32[32,32]{1,0:T(8,128)} %get-tuple-element.214) | copy-start | bytes 12292 | tf_op jit(solution)/shard_map/while
  111.8 10.8 %copy-start.2 = (f32[32,32]{1,0:T(8,128)S(1)}, f32[32,32]{1,0:T(8,128)}, u32[]{:S(2)}) copy-start(f32[32,32]{1,0:T(8,128)} %get-tuple-element.214) | copy-start | bytes 12292 | tf_op jit(solution)/shard_map/while
  159.8 10.8 %copy-start.2 = (f32[32,32]{1,0:T(8,128)S(1)}, f32[32,32]{1,0:T(8,128)}, u32[]{:S(2)}) copy-start(f32[32,32]{1,0:T(8,128)} %get-tuple-element.214) | copy-start | bytes 12292 | tf_op jit(solution)/shard_map/while
  251.6 59.9 %all-to-all-start.1 = ((f32[16,32,2,1024]{3,2,0,1:T(2,128)}), f32[16,32,2,1024]{3,2,0,1:T(2,128)}, u32[]{:S(2)}, u32[]{:S(2)}) async-start(f32[16,32,2,1024]{3,2,0,1:T(2,128)} %copy.191), calls=%async_computation.1 | async-start | bytes 8388608 | tf_op jit(solution)/shard_map/all_to_all | solution.py:128
  355.8 35.6 %all-to-all-start.2 = ((f32[2,1024,256]{2,0,1:T(2,128)}), f32[2,1024,256]{2,0,1:T(2,128)S(1)}, u32[]{:S(2)}, u32[]{:S(2)}) async-start(f32[2,1024,256]{2,0,1:T(2,128)} %reshape.240), calls=%async_computation.2 | async-start | bytes 4194304 | tf_op jit(solution)/shard_map/all_to_all | solution.py:139
  396.4 1.2 copy-start
  561.0 1.2 copy-start.1
where the time goes:
time: 587 us; the launch traced here: 582 us
  matrix products  198 us (34%)
  local copies, waits for them, and re-layouts  156 us (27%)
  blocking collectives  92.7 us (16%)
  waiting for transfers between devices  79.9 us (14%)
  other arithmetic  24.8 us (4%)
  starting transfers between devices  23.8 us (4%)
  loops' own time  6.23 us (1%)
    dot_general x16, matrix products, pairwise(): return jnp.einsum('nyv,nxv->nyx', first_arr, second_arr, precision=exact)  145 us
    all_to_all x1, blocking collectives, shards(): lax.all_to_all(flipped, 'band', split_axis=1, concat_axis=2, tiled=True)  60.2 us
    all_to_all x1, waiting for transfers between devices, shards(): lax.all_to_all(packed, 'base', split_axis=1, concat_axis=1, tiled=True)  51.9 us
    all_to_all x1, blocking collectives, shards(): lax.all_to_all(jnp.stack([row_re, row_im]), 'base', split_axis=2, concat_...  32.4 us
    all_to_all x1, waiting for transfers between devices, shards(): lax.all_to_all(uv_grid, 'base', split_axis=1, concat_axis=2, tiled=True)  28 us
    scatter x1, local copies, waits for them, and re-layouts, shards(): packed = jnp.zeros((buffer_len, 2, area), jnp.float32).at[target].set(tiles)  26.5 us
    unnamed x7, local copies, waits for them, and re-layouts  22.6 us
    reshape x2, local copies, waits for them, and re-layouts, shards(): uv_grid = uv_grid.reshape(2, row_tiles * extent, col_tiles * extent)  22 us
  transfers between devices with their start and end apart: 3, of which 2 were waited for; matrix products, arithmetic and copies ran while one was open for 40% of the time, Pallas kernels for 0%

commit v1 on v0

--- a/solution.py
+++ b/solution.py
@@ -138,8 +138,14 @@
     uv_grid = uv_grid.reshape(2, row_tiles * extent, col_tiles * extent)
     row_major = lax.all_to_all(uv_grid, "base", split_axis=1, concat_axis=2, tiled=True)
     row_re, row_im = dft_last(row_major[0], row_major[1])
-    returned = lax.all_to_all(
-        jnp.stack([row_re, row_im]), "base", split_axis=2, concat_axis=1, tiled=True
+    returned = jnp.concatenate(
+        lax.all_to_all(
+            jnp.stack(jnp.split(jnp.stack([row_re, row_im]), lax.axis_size("base"), axis=2)),
+            "base",
+            0,
+            0,
+        ),
+        axis=1,
     )
     flipped = jnp.transpose(returned, (0, 2, 1))
     col_major = lax.all_to_all(flipped, "band", split_axis=1, concat_axis=2, tiled=True)

time: 587 us -> 542 us (0.923)
  local copies, waits for them, and re-layouts: 156 us -> 121 us
  other arithmetic: 24.8 us -> 16.1 us
    unnamed x7 -> x37, local copies, waits for them, and re-layouts: 22.6 us -> 5.5 us
    all_to_all x2 -> x0, local copies, waits for them, and re-layouts: 10.2 us -> none  [shards(): lax.all_to_all(jnp.stack([row_re, row_im]), 'base', split_axis=2, concat_...]
    another operation x3, local copies, waits for them, and re-layouts: 11.8 us -> 3.99 us  [shards(): jnp.stack([row_re, row_im])]
    all_to_all x1 -> x0, other arithmetic: 7.39 us -> none  [shards(): lax.all_to_all(jnp.stack([row_re, row_im]), 'base', split_axis=2, concat_...]
  transfers between devices with their start and end apart: 3 -> 3, of which waited for: 2 -> 2; matrix products, arithmetic and copies ran while one was open for 40% -> 43% of each run, Pallas kernels for 0% -> 0%
where the time goes in v1:
time: 542 us; the launch traced here: 537 us
  matrix products  198 us (37%)
  local copies, waits for them, and re-layouts  121 us (22%)
  blocking collectives  91.6 us (17%)
  waiting for transfers between devices  79.9 us (15%)
  starting transfers between devices  24.1 us (4%)
  other arithmetic  16.1 us (3%)
  loops' own time  6.13 us (1%)
    dot_general x16, matrix products, pairwise(): return jnp.einsum('nyv,nxv->nyx', first_arr, second_arr, precision=exact)  145 us
    all_to_all x1, blocking collectives, shards(): lax.all_to_all(flipped, 'band', split_axis=1, concat_axis=2, tiled=True)  59.8 us
    all_to_all x1, waiting for transfers between devices, shards(): lax.all_to_all(packed, 'base', split_axis=1, concat_axis=1, tiled=True)  51.9 us
    all_to_all x1, blocking collectives, shards(): lax.all_to_all(jnp.stack(jnp.split(jnp.stack([row_re, row_im]), lax.axis_...  31.8 us
    all_to_all x1, waiting for transfers between devices, shards(): lax.all_to_all(uv_grid, 'base', split_axis=1, concat_axis=2, tiled=True)  28 us
    scatter x1, local copies, waits for them, and re-layouts, shards(): packed = jnp.zeros((buffer_len, 2, area), jnp.float32).at[target].set(tiles)  26.5 us
    reshape x2, local copies, waits for them, and re-layouts, shards(): uv_grid = uv_grid.reshape(2, row_tiles * extent, col_tiles * extent)  22 us
    dot_general x8, matrix products, mix_second(): return jnp.einsum('pkb,bm->pmk', values, table, precision=exact)  16.2 us
  transfers between devices with their start and end apart: 3, of which 2 were waited for; matrix products, arithmetic and copies ran while one was open for 43% of the time, Pallas kernels for 0%

profile of v1, /device:TPU:1, one launch (start us, length us, event | category | flops | bytes accessed | tf_op | source)
XLA Modules:
  0.0 537.4 jit_solution(10104104851454583800)
XLA Ops:
  3.6 1.4 scatter_custom_fusion
  5.8 8.6 %all-to-all-start = ((f32[16,32,1]{0,2,1:T(1,128)}), f32[16,32,1]{0,2,1:T(1,128)S(1)}, u32[]{:S(2)}, u32[]{:S(2)}) async-start(f32[16,32,1]{0,2,1:T(1,128)} %copy.182), calls=%async_computation | async-start | bytes 32768 | tf_op jit(solution)/shard_map/all_to_all | solution.py:129
  15.2 196.7 %while.12 = (s32[]{:T(128)}, f32[4,64,2,1024]{3,1,0,2:T(8,128)}, f32[4,64,2,128]{3,2,1,0:T(2,128)}, f32[4,64,2,8]{1,0,3,2:T(4,128)S(1)}, f32[16]{0:T(128)}, /*index=5*/f32[32,32]{1,0:T(8,128)}, s32[]{:T(128)}) while((s32[]{:T(128)}, f32[4,64,2,1024]{3,1,0,2:T(8,128)}, f32[4,64,2,128]{3,2,1,0:T(2,128)}, f32[4,64,2,8]{1,0,3,2:T(4,128)S(1)}, ...), condition=%wide.region_5.6_spmd, body=%wide.region_4.5_spmd.sunk | while | flops 610140224 | bytes 13221169 | solution.py:67
  17.3 8.9 %fusion.319 = f32[64,32,32]{2,1,0:T(8,128)S(1)} fusion(f32[64,128]{1,0:T(8,128)S(1)} %copy.242, f32[64,128]{1,0:T(8,128)S(1)} %get-tuple-element.192, f32[64,128]{1,0:T(8,128)S(1)} %copy.244, f32[32]{0:T(128)S(1)} %add_multiply_fusion.2, f32[64,128]{1,0:T(8,128)S(1)} %get-tuple-element.194), kind=kOutput, calls=%fused_computation.12.clone.1 | convolution fusion | flops 101974016 | bytes 393344 | tf_op jit(solution)/shard_map/while/body/eval_jaxpr/nyv,nxv->nyx/dot_general | solution.py:39
  26.2 9.1 %fusion.320 = f32[64,32,32]{2,1,0:T(8,128)S(1)} fusion(f32[64,32,32]{2,1,0:T(8,128)S(1)} %fusion.319, f32[32,32]{1,0:T(8,128)S(1)} %copy-done.2, f32[64,128]{1,0:T(8,128)S(1)} %copy.242, f32[64,128]{1,0:T(8,128)S(1)} %get-tuple-element.192, f32[64,128]{1,0:T(8,128)S(1)} %copy.244, f32[32]{0:T(128)S(1)} %add_multiply_fusion.2, ...), kind=kOutput, calls=%fused_computation.18.clone.1 | convolution fusion | flops 102105088 | bytes 659584 | tf_op jit(solution)/shard_map/while/body/eval_jaxpr/nyv,nxv->nyx/dot_general | solution.py:39
  36.5 9.3 %fusion.316 = f32[64,32,32]{2,1,0:T(8,128)S(1)} fusion(f32[64,128]{1,0:T(8,128)S(1)} %copy.242, f32[64,128]{1,0:T(8,128)S(1)} %get-tuple-element.192, f32[64,128]{1,0:T(8,128)S(1)} %copy.244, f32[32]{0:T(128)S(1)} %add_multiply_fusion.2, f32[64,128]{1,0:T(8,128)S(1)} %get-tuple-element.194), kind=kOutput, calls=%fused_computation.11.clone.1 | convolution fusion | flops 101974016 | bytes 393344 | tf_op jit(solution)/shard_map/while/body/eval_jaxpr/nyv,nxv->nyx/dot_general | solution.py:39
  45.8 9.1 %fusion.317 = f32[64,32,32]{2,1,0:T(8,128)S(1)} fusion(f32[64,32,32]{2,1,0:T(8,128)S(1)} %fusion.316, f32[32,32]{1,0:T(8,128)S(1)} %copy-done.2, f32[64,128]{1,0:T(8,128)S(1)} %copy.242, f32[64,128]{1,0:T(8,128)S(1)} %get-tuple-element.192, f32[64,128]{1,0:T(8,128)S(1)} %copy.244, f32[32]{0:T(128)S(1)} %add_multiply_fusion.2, ...), kind=kOutput, calls=%fused_computation.17.clone.1 | convolution fusion | flops 102105088 | bytes 659584 | tf_op jit(solution)/shard_map/while/body/eval_jaxpr/nyv,nxv->nyx/dot_general | solution.py:39
  59.7 0.9 fusion.321
  65.3 8.9 %fusion.319 = f32[64,32,32]{2,1,0:T(8,128)S(1)} fusion(f32[64,128]{1,0:T(8,128)S(1)} %copy.242, f32[64,128]{1,0:T(8,128)S(1)} %get-tuple-element.192, f32[64,128]{1,0:T(8,128)S(1)} %copy.244, f32[32]{0:T(128)S(1)} %add_multiply_fusion.2, f32[64,128]{1,0:T(8,128)S(1)} %get-tuple-element.194), kind=kOutput, calls=%fused_computation.12.clone.1 | convolution fusion | flops 101974016 | bytes 393344 | tf_op jit(solution)/shard_map/while/body/eval_jaxpr/nyv,nxv->nyx/dot_general | solution.py:39
  74.2 9.3 %fusion.320 = f32[64,32,32]{2,1,0:T(8,128)S(1)} fusion(f32[64,32,32]{2,1,0:T(8,128)S(1)} %fusion.319, f32[32,32]{1,0:T(8,128)S(1)} %copy-done.2, f32[64,128]{1,0:T(8,128)S(1)} %copy.242, f32[64,128]{1,0:T(8,128)S(1)} %get-tuple-element.192, f32[64,128]{1,0:T(8,128)S(1)} %copy.244, f32[32]{0:T(128)S(1)} %add_multiply_fusion.2, ...), kind=kOutput, calls=%fused_computation.18.clone.1 | convolution fusion | flops 102105088 | bytes 659584 | tf_op jit(solution)/shard_map/while/body/eval_jaxpr/nyv,nxv->nyx/dot_general | solution.py:39
  84.7 9.0 %fusion.316 = f32[64,32,32]{2,1,0:T(8,128)S(1)} fusion(f32[64,128]{1,0:T(8,128)S(1)} %copy.242, f32[64,128]{1,0:T(8,128)S(1)} %get-tuple-element.192, f32[64,128]{1,0:T(8,128)S(1)} %copy.244, f32[32]{0:T(128)S(1)} %add_multiply_fusion.2, f32[64,128]{1,0:T(8,128)S(1)} %get-tuple-element.194), kind=kOutput, calls=%fused_computation.11.clone.1 | convolution fusion | flops 101974016 | bytes 393344 | tf_op jit(solution)/shard_map/while/body/eval_jaxpr/nyv,nxv->nyx/dot_general | solution.py:39
  93.8 9.1 %fusion.317 = f32[64,32,32]{2,1,0:T(8,128)S(1)} fusion(f32[64,32,32]{2,1,0:T(8,128)S(1)} %fusion.316, f32[32,32]{1,0:T(8,128)S(1)} %copy-done.2, f32[64,128]{1,0:T(8,128)S(1)} %copy.242, f32[64,128]{1,0:T(8,128)S(1)} %get-tuple-element.192, f32[64,128]{1,0:T(8,128)S(1)} %copy.244, f32[32]{0:T(128)S(1)} %add_multiply_fusion.2, ...), kind=kOutput, calls=%fused_computation.17.clone.1 | convolution fusion | flops 102105088 | bytes 659584 | tf_op jit(solution)/shard_map/while/body/eval_jaxpr/nyv,nxv->nyx/dot_general | solution.py:39
  107.7 0.9 fusion.321
  113.5 8.9 %fusion.319 = f32[64,32,32]{2,1,0:T(8,128)S(1)} fusion(f32[64,128]{1,0:T(8,128)S(1)} %copy.242, f32[64,128]{1,0:T(8,128)S(1)} %get-tuple-element.192, f32[64,128]{1,0:T(8,128)S(1)} %copy.244, f32[32]{0:T(128)S(1)} %add_multiply_fusion.2, f32[64,128]{1,0:T(8,128)S(1)} %get-tuple-element.194), kind=kOutput, calls=%fused_computation.12.clone.1 | convolution fusion | flops 101974016 | bytes 393344 | tf_op jit(solution)/shard_map/while/body/eval_jaxpr/nyv,nxv->nyx/dot_general | solution.py:39
  122.4 9.1 %fusion.320 = f32[64,32,32]{2,1,0:T(8,128)S(1)} fusion(f32[64,32,32]{2,1,0:T(8,128)S(1)} %fusion.319, f32[32,32]{1,0:T(8,128)S(1)} %copy-done.2, f32[64,128]{1,0:T(8,128)S(1)} %copy.242, f32[64,128]{1,0:T(8,128)S(1)} %get-tuple-element.192, f32[64,128]{1,0:T(8,128)S(1)} %copy.244, f32[32]{0:T(128)S(1)} %add_multiply_fusion.2, ...), kind=kOutput, calls=%fused_computation.18.clone.1 | convolution fusion | flops 102105088 | bytes 659584 | tf_op jit(solution)/shard_map/while/body/eval_jaxpr/nyv,nxv->nyx/dot_general | solution.py:39
  132.7 9.1 %fusion.316 = f32[64,32,32]{2,1,0:T(8,128)S(1)} fusion(f32[64,128]{1,0:T(8,128)S(1)} %copy.242, f32[64,128]{1,0:T(8,128)S(1)} %get-tuple-element.192, f32[64,128]{1,0:T(8,128)S(1)} %copy.244, f32[32]{0:T(128)S(1)} %add_multiply_fusion.2, f32[64,128]{1,0:T(8,128)S(1)} %get-tuple-element.194), kind=kOutput, calls=%fused_computation.11.clone.1 | convolution fusion | flops 101974016 | bytes 393344 | tf_op jit(solution)/shard_map/while/body/eval_jaxpr/nyv,nxv->nyx/dot_general | solution.py:39
  141.8 9.3 %fusion.317 = f32[64,32,32]{2,1,0:T(8,128)S(1)} fusion(f32[64,32,32]{2,1,0:T(8,128)S(1)} %fusion.316, f32[32,32]{1,0:T(8,128)S(1)} %copy-done.2, f32[64,128]{1,0:T(8,128)S(1)} %copy.242, f32[64,128]{1,0:T(8,128)S(1)} %get-tuple-element.192, f32[64,128]{1,0:T(8,128)S(1)} %copy.244, f32[32]{0:T(128)S(1)} %add_multiply_fusion.2, ...), kind=kOutput, calls=%fused_computation.17.clone.1 | convolution fusion | flops 102105088 | bytes 659584 | tf_op jit(solution)/shard_map/while/body/eval_jaxpr/nyv,nxv->nyx/dot_general | solution.py:39
  161.5 8.9 %fusion.319 = f32[64,32,32]{2,1,0:T(8,128)S(1)} fusion(f32[64,128]{1,0:T(8,128)S(1)} %copy.242, f32[64,128]{1,0:T(8,128)S(1)} %get-tuple-element.192, f32[64,128]{1,0:T(8,128)S(1)} %copy.244, f32[32]{0:T(128)S(1)} %add_multiply_fusion.2, f32[64,128]{1,0:T(8,128)S(1)} %get-tuple-element.194), kind=kOutput, calls=%fused_computation.12.clone.1 | convolution fusion | flops 101974016 | bytes 393344 | tf_op jit(solution)/shard_map/while/body/eval_jaxpr/nyv,nxv->nyx/dot_general | solution.py:39
  170.4 9.1 %fusion.320 = f32[64,32,32]{2,1,0:T(8,128)S(1)} fusion(f32[64,32,32]{2,1,0:T(8,128)S(1)} %fusion.319, f32[32,32]{1,0:T(8,128)S(1)} %copy-done.2, f32[64,128]{1,0:T(8,128)S(1)} %copy.242, f32[64,128]{1,0:T(8,128)S(1)} %get-tuple-element.192, f32[64,128]{1,0:T(8,128)S(1)} %copy.244, f32[32]{0:T(128)S(1)} %add_multiply_fusion.2, ...), kind=kOutput, calls=%fused_computation.18.clone.1 | convolution fusion | flops 102105088 | bytes 659584 | tf_op jit(solution)/shard_map/while/body/eval_jaxpr/nyv,nxv->nyx/dot_general | solution.py:39
  180.8 9.3 %fusion.316 = f32[64,32,32]{2,1,0:T(8,128)S(1)} fusion(f32[64,128]{1,0:T(8,128)S(1)} %copy.242, f32[64,128]{1,0:T(8,128)S(1)} %get-tuple-element.192, f32[64,128]{1,0:T(8,128)S(1)} %copy.244, f32[32]{0:T(128)S(1)} %add_multiply_fusion.2, f32[64,128]{1,0:T(8,128)S(1)} %get-tuple-element.194), kind=kOutput, calls=%fused_computation.11.clone.1 | convolution fusion | flops 101974016 | bytes 393344 | tf_op jit(solution)/shard_map/while/body/eval_jaxpr/nyv,nxv->nyx/dot_general | solution.py:39
  190.0 9.1 %fusion.317 = f32[64,32,32]{2,1,0:T(8,128)S(1)} fusion(f32[64,32,32]{2,1,0:T(8,128)S(1)} %fusion.316, f32[32,32]{1,0:T(8,128)S(1)} %copy-done.2, f32[64,128]{1,0:T(8,128)S(1)} %copy.242, f32[64,128]{1,0:T(8,128)S(1)} %get-tuple-element.192, f32[64,128]{1,0:T(8,128)S(1)} %copy.244, f32[32]{0:T(128)S(1)} %add_multiply_fusion.2, ...), kind=kOutput, calls=%fused_computation.17.clone.1 | convolution fusion | flops 102105088 | bytes 659584 | tf_op jit(solution)/shard_map/while/body/eval_jaxpr/nyv,nxv->nyx/dot_general | solution.py:39
  211.9 3.2 copy.188
  215.1 3.0 broadcast_in_dim.11
  218.2 26.5 %scatter_fusion = f32[512,2,1024]{2,1,0:T(2,128)} fusion(f32[512,2,1024]{2,1,0:T(2,128)} %broadcast_in_dim.11, s32[256]{0:T(256)S(1)} %bitcast.362, f32[256,2,1024]{2,1,0:T(2,128)S(1)} %copy.188), kind=kCustom, calls=%fused_computation.1 | custom fusion | bytes 6292480 | tf_op jit(solution)/shard_map/scatter | solution.py:125
  244.7 6.6 %copy.189 = f32[16,32,2,1024]{3,2,0,1:T(2,128)} copy(f32[16,32,2,1024]{3,2,1,0:T(2,128)} %bitcast.347) | data formatting | bytes 8388608 | tf_op jit(solution)/shard_map/reshape | solution.py:126
  251.4 7.8 %all-to-all-start.1 = ((f32[16,32,2,1024]{3,2,0,1:T(2,128)}), f32[16,32,2,1024]{3,2,0,1:T(2,128)}, u32[]{:S(2)}, u32[]{:S(2)}) async-start(f32[16,32,2,1024]{3,2,0,1:T(2,128)} %copy.189), calls=%async_computation.1 | async-start | bytes 8388608 | tf_op jit(solution)/shard_map/all_to_all | solution.py:128
  259.3 51.9 %all-to-all-done.1 = f32[16,32,2,1024]{3,2,0,1:T(2,128)} async-done(((f32[16,32,2,1024]{3,2,0,1:T(2,128)}), f32[16,32,2,1024]{3,2,0,1:T(2,128)}, u32[]{:S(2)}, u32[]{:S(2)}) %all-to-all-start.1) | async-done | bytes 4194336 | tf_op jit(solution)/shard_map/all_to_all | solution.py:128
  311.2 4.3 copy.190
  315.5 3.9 copy.214
  319.4 8.9 %scatter_custom_fusion.2 = f32[256,2048]{1,0:T(8,128)S(1)} fusion(s32[512]{0:T(512)S(1)} %reshape.235, f32[512,2048]{1,0:T(8,128)} %bitcast.354, f32[]{:T(128)} %constant.129.clone.1), kind=kCustom, calls=%fused_computation.147 | custom fusion | flops 1048576 | bytes 2097664 | tf_op jit(solution)/shard_map/scatter-add | solution.py:134
  328.4 5.0 reshape.213
  333.4 14.3 %copy.207 = f32[2,32,32,8,32]{4,3,0,2,1:T(8,128)} copy(f32[2,32,32,8,32]{4,2,0,3,1:T(8,128)} %bitcast.346) | data formatting | bytes 4194304 | tf_op jit(solution)/shard_map/reshape | solution.py:138
  347.6 7.7 %reshape.248 = f32[2,1024,256]{2,0,1:T(2,128)} reshape(f32[2,32,32,8,32]{4,3,0,2,1:T(8,128)} %copy.207) | data formatting | bytes 4194304 | tf_op jit(solution)/shard_map/reshape | solution.py:138
  355.4 7.7 %all-to-all-start.2 = ((f32[2,1024,256]{2,0,1:T(2,128)}), f32[2,1024,256]{2,0,1:T(2,128)S(1)}, u32[]{:S(2)}, u32[]{:S(2)}) async-start(f32[2,1024,256]{2,0,1:T(2,128)} %reshape.248), calls=%async_computation.2 | async-start | bytes 4194304 | tf_op jit(solution)/shard_map/all_to_all | solution.py:139
  363.2 28.0 %all-to-all-done.2 = f32[2,1024,256]{2,0,1:T(2,128)S(1)} async-done(((f32[2,1024,256]{2,0,1:T(2,128)}), f32[2,1024,256]{2,0,1:T(2,128)S(1)}, u32[]{:S(2)}, u32[]{:S(2)}) %all-to-all-start.2) | async-done | bytes 2097184 | tf_op jit(solution)/shard_map/all_to_all | solution.py:139
  392.3 1.2 fusion.155
  393.4 2.1 fusion.148
  396.3 1.2 convolution_subtract_fusion.5
  397.5 1.2 convolution_add_fusion.5
  398.7 1.2 fusion.116
  399.9 2.2 fusion.118
  402.1 1.2 fusion.106
  403.4 1.9 copy.197
  405.3 2.3 stack_reshape.13
  407.6 3.4 fusion.107
  411.0 1.8 copy.196
  412.9 1.6 stack_reshape.12
  414.5 1.3 constant_dynamic-update-slice_fusion.2
  416.4 31.8 %all_to_all.49 = f32[32,2,32,256]{3,2,1,0:T(8,128)S(1)} all-to-all(f32[32,2,32,256]{3,2,1,0:T(8,128)S(1)} %constant_dynamic-update-slice_fusion.3), channel_id=1, replica_groups=mesh['base'=32,'band'=8] {'base'}, dimensions={0} | all-to-all | bytes 4194304 | tf_op jit(solution)/shard_map/all_to_all | solution.py:142
  448.3 2.3 copy.199
  450.6 59.8 %all_to_all.50 = f32[2,256,1024]{2,0,1:T(2,128)S(1)} all-to-all(f32[2,256,1024]{2,0,1:T(2,128)} %copy.199), channel_id=1, replica_groups=mesh['base'=32,'band'=8] {'band'}, dimensions={1} | all-to-all | bytes 4194304 | tf_op jit(solution)/shard_map/all_to_all | solution.py:151
  512.2 1.2 fusion.152
  513.3 2.1 fusion.145
  516.3 1.2 convolution_subtract_fusion.3
  517.5 1.2 convolution_add_fusion.3
  518.6 1.2 fusion.112
  519.9 2.2 fusion.110
  522.1 1.2 fusion.105
  523.3 1.9 copy.203
  525.3 2.3 stack_reshape.14
  527.6 3.4 fusion.104
  531.0 1.8 copy.204
  532.9 1.6 stack_reshape.15
  534.5 2.7 maximum_multiply_fusion.1
  (178 shorter events, 53.7 us)
Async XLA Ops:
  5.8 245.6 %all-to-all-start = ((f32[16,32,1]{0,2,1:T(1,128)}), f32[16,32,1]{0,2,1:T(1,128)S(1)}, u32[]{:S(2)}, u32[]{:S(2)}) async-start(f32[16,32,1]{0,2,1:T(1,128)} %copy.182), calls=%async_computation | async-start | bytes 32768 | tf_op jit(solution)/shard_map/all_to_all | solution.py:129
  15.4 10.8 %copy-start.2 = (f32[32,32]{1,0:T(8,128)S(1)}, f32[32,32]{1,0:T(8,128)}, u32[]{:S(2)}) copy-start(f32[32,32]{1,0:T(8,128)} %get-tuple-element.214) | copy-start | bytes 12292 | tf_op jit(solution)/shard_map/while
  63.4 10.8 %copy-start.2 = (f32[32,32]{1,0:T(8,128)S(1)}, f32[32,32]{1,0:T(8,128)}, u32[]{:S(2)}) copy-start(f32[32,32]{1,0:T(8,128)} %get-tuple-element.214) | copy-start | bytes 12292 | tf_op jit(solution)/shard_map/while
  111.6 10.8 %copy-start.2 = (f32[32,32]{1,0:T(8,128)S(1)}, f32[32,32]{1,0:T(8,128)}, u32[]{:S(2)}) copy-start(f32[32,32]{1,0:T(8,128)} %get-tuple-element.214) | copy-start | bytes 12292 | tf_op jit(solution)/shard_map/while
  159.6 10.8 %copy-start.2 = (f32[32,32]{1,0:T(8,128)S(1)}, f32[32,32]{1,0:T(8,128)}, u32[]{:S(2)}) copy-start(f32[32,32]{1,0:T(8,128)} %get-tuple-element.214) | copy-start | bytes 12292 | tf_op jit(solution)/shard_map/while
  251.4 59.8 %all-to-all-start.1 = ((f32[16,32,2,1024]{3,2,0,1:T(2,128)}), f32[16,32,2,1024]{3,2,0,1:T(2,128)}, u32[]{:S(2)}, u32[]{:S(2)}) async-start(f32[16,32,2,1024]{3,2,0,1:T(2,128)} %copy.189), calls=%async_computation.1 | async-start | bytes 8388608 | tf_op jit(solution)/shard_map/all_to_all | solution.py:128
  355.4 35.9 %all-to-all-start.2 = ((f32[2,1024,256]{2,0,1:T(2,128)}), f32[2,1024,256]{2,0,1:T(2,128)S(1)}, u32[]{:S(2)}, u32[]{:S(2)}) async-start(f32[2,1024,256]{2,0,1:T(2,128)} %reshape.248), calls=%async_computation.2 | async-start | bytes 4194304 | tf_op jit(solution)/shard_map/all_to_all | solution.py:139
  396.3 1.2 copy-start
  516.2 1.2 copy-start.1
